TPU v7x, 512 devices: a whole 4x4x16 slice. The times are simulated.
512 devices in a mesh: section: 8 (over z_lo, core), mp: 64 (over x, z_hi, y).
Axes of the slice: x: 4, y: 4, z: 16 (z_hi: 4, z_lo: 4; z = z_hi * 4 + z_lo), core: 2. Of those that a mesh axis runs over, the one named last changes fastest.
Arguments:
- pending_vectors: bfloat16 [8, 128, 3584], P('section', None, 'mp'), may hold values from -6 to 6
- arriving_learner_vectors: bfloat16 [1, 128, 3584], P(None, None, 'mp'), may hold values from -6 to 6
- mentor_state_vectors: bfloat16 [64, 2, 128, 8192], P('section', None, None, 'mp'), may hold values from -6 to 6
- breadth_mapping_matrix: bfloat16 [8192, 3584], P('mp', 'section'), may hold values from -0.0625 to 0.0625
- rms_gain_factor: float32 [8, 3584], P('section'), may hold values from 0.25 to 1.75
- gating_matrix: bfloat16 [8, 3584, 9472], P('section', None, 'mp'), may hold values from -0.09375 to 0.09375
- lowering_matrix: bfloat16 [8, 9472, 3584], P('section', 'mp'), may hold values from -0.0625 to 0.0625
- mentor_depth_table: int32 [8], replicated, may hold values from 0 to 63, as said below
Outputs:
- grad_gate: bfloat16 [8, 3584, 9472], P('section', None, 'mp')
- grad_down: bfloat16 [8, 9472, 3584], P('section', 'mp')
- distill_loss: float32 [], replicated
Inputs may be any that keep to these rules, and one draw needn't show every extreme that they name: `mentor_depth_table`: the entries are distinct teacher depths.
All inputs are finite; a program needn't handle non-finite values.
Results may differ from a plain program's by a relative error of at most 0.011.
Values may be sent and summed in bfloat16 or wider, within the bound.
A program may use at most 64 MiB of HBM per device.

v0:
```python
import jax
import jax.numpy as jnp
from jax import lax
from jax.sharding import PartitionSpec as P


def shifted(shard, axis, by):
    peers = lax.axis_size(axis)
    pairs = [(i, i + by) for i in range(peers) if 0 <= i + by < peers]
    return lax.ppermute(shard, axis, pairs)


def normalize(held, gain):
    values = held.astype(jnp.float32)
    spread = jnp.mean(values * values, axis=-1, keepdims=True)
    return (values * lax.rsqrt(spread + 1e-06) * gain).astype(jnp.bfloat16)


def project_share(teacher_block, breadth_mapping_matrix):
    partial_sum = jnp.dot(
        teacher_block,
        lax.all_gather(breadth_mapping_matrix, "section", axis=1, tiled=True),
        preferred_element_type=jnp.float32,
    )
    return lax.psum_scatter(partial_sum, "mp", scatter_dimension=1, tiled=True)


def local(
    pending_vectors,
    arriving_learner_vectors,
    mentor_state_vectors,
    breadth_mapping_matrix,
    rms_gain_factor,
    gating_matrix,
    lowering_matrix,
    mentor_depth_table,
):
    sections = lax.axis_size("section")
    ticks = arriving_learner_vectors.shape[0] + 1
    overall_entry_tally = pending_vectors.shape[1]
    width = gating_matrix.shape[1]
    local_depths = mentor_state_vectors.shape[0]
    part_index = lax.axis_index("section")
    positions = jnp.arange(sections, dtype=jnp.int32)
    picked = jnp.sum(jnp.where(positions == part_index, mentor_depth_table, 0))
    depth_ids = jnp.arange(sections * local_depths, dtype=jnp.int32)
    selector = (depth_ids == picked).astype(jnp.bfloat16)
    teacher_local = mentor_state_vectors.reshape(
        local_depths, ticks * overall_entry_tally, mentor_state_vectors.shape[3]
    )
    every_rows = lax.all_gather(teacher_local, "section", axis=0, tiled=True)
    chosen = jnp.einsum(
        "s,srk->rk", selector, every_rows, preferred_element_type=jnp.float32
    ).astype(jnp.bfloat16)
    share = project_share(chosen, breadth_mapping_matrix).astype(jnp.bfloat16)
    is_opening = jnp.concatenate([pending_vectors, arriving_learner_vectors], axis=0)
    entering = lax.all_gather(is_opening, "mp", axis=2, tiled=True)
    held = entering[0]
    gain = rms_gain_factor[0]
    gate_local = gating_matrix[0]
    down_local = lowering_matrix[0]
    gate_acc = jnp.zeros(gate_local.shape, jnp.float32)
    down_acc = jnp.zeros(down_local.shape, jnp.float32)
    objective = jnp.zeros((), jnp.float32)
    target = lax.all_gather(share, "mp", axis=1, tiled=True).reshape(
        ticks, overall_entry_tally, width
    )
    for moment in range(ticks):
        normed = normalize(held, gain)
        gate_sum = jnp.dot(normed, gate_local, preferred_element_type=jnp.float32)
        activated = jax.nn.silu(gate_sum).astype(jnp.bfloat16)
        partial_out = jnp.dot(activated, down_local, preferred_element_type=jnp.float32)
        mixed = lax.psum(partial_out, "mp")
        output = (held.astype(jnp.float32) + mixed).astype(jnp.bfloat16)
        differ = output.astype(jnp.float32) - target[moment].astype(jnp.float32)
        objective = objective + jnp.sum(differ * differ) / (2.0 * overall_entry_tally)
        delta = (differ / overall_entry_tally).astype(jnp.bfloat16)
        down_acc = down_acc + jnp.dot(activated.T, delta, preferred_element_type=jnp.float32)
        back = jnp.dot(delta, down_local.T, preferred_element_type=jnp.float32)
        sigma = jax.nn.sigmoid(gate_sum)
        slope = (back * sigma * (1.0 + gate_sum * (1.0 - sigma))).astype(jnp.bfloat16)
        gate_acc = gate_acc + jnp.dot(normed.T, slope, preferred_element_type=jnp.float32)
        if moment + 1 < ticks:
            passed = shifted(output, "section", 1)
            held = jnp.where(part_index == 0, entering[moment + 1], passed)
    total = lax.psum(objective, "section")
    distill_loss = total / (sections * ticks * width)
    return (gate_acc.astype(jnp.bfloat16)[None], down_acc.astype(jnp.bfloat16)[None], distill_loss)


def solution(mesh):
    in_specs = (
        P("section", None, "mp"),
        P(None, None, "mp"),
        P("section", None, None, "mp"),
        P("mp", "section"),
        P("section", None),
        P("section", None, "mp"),
        P("section", "mp", None),
        P(),
    )
    out_specs = (P("section", None, "mp"), P("section", "mp", None), P())
    return jax.shard_map(local, mesh=mesh, in_specs=in_specs, out_specs=out_specs, check_vma=False)
```

profile of v0, /device:TPU:1, one launch (start us, length us, event | category | flops | bytes accessed | tf_op | source)
XLA Modules:
  0.0 2483.9 jit_solution(2435663147152228064)
XLA Ops:
  7.2 0.7 all-gather.6.cloned.1.call-update
  8.0 1.3 fusion.58
  9.3 22.9 all_gather.14
  32.1 40.8 %all-gather.6.cloned.1.call-done = bf16[64,256,128]{2,1,0:T(8,128)(2,1)} async-done(((bf16[8,256,128]{2,1,0:T(8,128)(2,1)}), bf16[64,256,128]{2,1,0:T(8,128)(2,1)}) %all-gather.6.cloned.1.call-update) | async-done | bytes 4194320 | tf_op jit(solution)/shard_map/all_gather | solution.py:51
  72.9 5.2 fusion.4
  78.1 2.4 convolution_bitcast_fusion
  81.9 404.2 %reduce-scatter.4.cloned.1.call-done = f32[56,256]{1,0:T(8,128)} async-done(((f32[3584,256]{1,0:T(8,128)}), f32[56,256]{1,0:T(8,128)}) %reduce-scatter.4.cloned.1.call-update) | async-done | bytes 57360
  486.1 1.4 bitcast_convert_fusion
  487.7 156.0 %all-gather.4.cloned.1.call-done = bf16[2,128,3584]{1,0,2:T(2,128)(2,1)} async-done(((bf16[2,128,56]{1,0,2:T(2,128)(2,1)}), bf16[2,128,3584]{1,0,2:T(2,128)(2,1)}) %all-gather.4.cloned.1.call-update) | async-done | bytes 1835024 | tf_op jit(solution)/shard_map/all_gather | solution.py:57
  643.7 6.2 fusion.72
  649.9 3.8 copy.33
  654.0 1.8 fusion.33
  655.8 1.7 fusion.29
  657.6 98.0 %all-gather.8.cloned.1.call-done = bf16[256,3584]{0,1:T(8,128)(2,1)} async-done(((bf16[256,56]{0,1:T(8,128)(2,1)}), bf16[256,3584]{0,1:T(8,128)(2,1)}) %all-gather.8.cloned.1.call-update) | async-done | bytes 1835024 | tf_op jit(solution)/shard_map/all_gather | solution.py:65
  755.6 2.8 fusion.71
  758.4 1.5 copy.34
  759.9 790.1 %all-reduce.3.cloned.1.call-done = f32[128,3584]{1,0:T(8,128)} async-done(((f32[128,3584]{1,0:T(8,128)}), f32[128,3584]{1,0:T(8,128)}) %all-reduce.3.cloned.1.call-update) | async-done | bytes 1835024 | tf_op jit(solution)/shard_map/psum | solution.py:73
  1550.0 3.5 multiply_reduce_fusion.1
  1553.5 45.1 %collective-permute-start = (bf16[128,3584]{1,0:T(8,128)(2,1)}, bf16[128,3584]{1,0:T(8,128)(2,1)}, u32[]{:S(2)}, u32[]{:S(2)}) collective-permute-start(bf16[128,3584]{1,0:T(8,128)(2,1)} %get-tuple-element.6), channel_id=1, source_target_pairs={{0,64},{64,128},{128,192},{192,256},{256,320},{320,384},{384,448},... | collective-permute-start | bytes 2752520 | tf_op jit(solution)/shard_map/ppermute | solution.py:10
  1598.6 3.8 copy.35
  1602.4 6.8 collective-permute-done
  1609.2 1.6 fusion.15
  1610.8 0.9 copy-done.2
  1612.3 1.7 fusion.25
  1614.1 1.5 copy.36
  1615.5 4.2 fusion.23
  1619.7 782.3 %all-reduce.5.cloned.1.call-done = f32[128,3584]{1,0:T(8,128)} async-done(((f32[128,3584]{1,0:T(8,128)}), f32[128,3584]{1,0:T(8,128)}) %all-reduce.5.cloned.1.call-update) | async-done | bytes 1835024 | tf_op jit(solution)/shard_map/psum | solution.py:73
  2402.0 3.7 multiply_reduce_fusion
  2407.0 3.0 fusion.46
  2410.0 57.4 %psum.23 = f32[]{:T(128)} all-reduce(f32[]{:T(128)S(6)} %add.65), channel_id=1, replica_groups=mesh['section'=8,'mp'=64] {'section'}, use_global_device_ids=true, to_apply=%region_8.9 | all-reduce | flops 1 | bytes 8 | tf_op jit(solution)/shard_map/psum | solution.py:86
  2467.5 3.5 fusion.2
  2471.0 4.3 fusion.3
  (33 shorter events, 2.5 us)
Async XLA Ops:
  7.2 648.6 %copy-start = (bf16[1,148,3584]{2,1,0:T(8,128)(2,1)S(1)}, bf16[1,148,3584]{2,1,0:T(8,128)(2,1)}, u32[]{:S(2)}) copy-start(bf16[1,148,3584]{2,1,0:T(8,128)(2,1)} %param.14) | copy-start | bytes 3182596
  7.2 65.7 %all-gather.6.cloned.1.call-start = ((), (), s32[]{:S(2)}) async-start(), calls=%async_computation.3 | async-start | bytes 4718592 | tf_op jit(solution)/shard_map/all_gather | solution.py:51
  7.9 478.2 %reduce-scatter.4.cloned.1.call-start = ((), (), s32[]{:S(2)}) async-start(), calls=%async_computation.6 | async-start | bytes 3727360
  80.5 0.7 copy-start.4
  80.5 0.7 copy-start.5
  80.5 407.2 %copy-start.6 = (f32[1,3584]{1,0:T(1,128)S(1)}, f32[1,3584]{1,0:T(1,128)}, u32[]{:S(2)}) copy-start(f32[1,3584]{1,0:T(1,128)} %param.12) | copy-start | bytes 43012
  80.5 563.2 %all-gather.4.cloned.1.call-start = ((), (), s32[]{:S(2)}) async-start(), calls=%async_computation.1 | async-start | bytes 1863680 | tf_op jit(solution)/shard_map/all_gather | solution.py:57
  81.9 673.8 %all-gather.8.cloned.1.call-start = ((), (), s32[]{:S(2)}) async-start(), calls=%async_computation.4 | async-start | bytes 1863680 | tf_op jit(solution)/shard_map/all_gather | solution.py:65
  487.6 1062.4 %all-reduce.3.cloned.1.call-start = ((), (), s32[]{:S(2)}) async-start(), calls=%async_computation.2 | async-start | bytes 3670016 | tf_op jit(solution)/shard_map/psum | solution.py:73
  653.7 896.3 %copy-start.1 = (bf16[1,128,3584]{2,1,0:T(8,128)(2,1)}, bf16[1,128,3584]{2,1,0:T(8,128)(2,1)S(1)}, u32[]{:S(2)}) copy-start(bf16[1,128,3584]{2,1,0:T(8,128)(2,1)S(1)} %copy.33) | copy-start | bytes 2752516
  657.6 1744.5 %all-reduce.5.cloned.1.call-start = ((), (), s32[]{:S(2)}) async-start(), calls=%async_computation.5 | async-start | bytes 3670016 | tf_op jit(solution)/shard_map/psum | solution.py:73
  1553.5 55.7 %collective-permute-start = (bf16[128,3584]{1,0:T(8,128)(2,1)}, bf16[128,3584]{1,0:T(8,128)(2,1)}, u32[]{:S(2)}, u32[]{:S(2)}) collective-permute-start(bf16[128,3584]{1,0:T(8,128)(2,1)} %get-tuple-element.6), channel_id=1, source_target_pairs={{0,64},{64,128},{128,192},{192,256},{256,320},{320,384},{384,448},... | collective-permute-start | bytes 2752520 | tf_op jit(solution)/shard_map/ppermute | solution.py:10
  1602.4 9.4 copy-start.7
  1610.8 0.9 copy-start.2
  2467.5 3.5 copy-start.3
Sparse Core Ops, SparseCore 0:
  10.1 62.7 all-gather.5
  80.6 405.4 reduce-scatter.3
  491.6 151.9 all-gather.3
  649.0 106.5 all-gather.7
  758.7 791.2 all-reduce.2
  1614.2 787.7 all-reduce.4
where the time goes:
time: 2480 us
  waiting for transfers between devices  2280 us (92%)
  blocking collectives  80.3 us (3%)
  starting transfers between devices  45.3 us (2%)
  matrix products  28.4 us (1%)
    psum x2, waiting for transfers between devices, local(): mixed = lax.psum(partial_out, 'mp')  1570 us
    unnamed x7, waiting for transfers between devices  405 us
    all_gather x1, waiting for transfers between devices, local(): entering = lax.all_gather(is_opening, 'mp', axis=2, tiled=True)  156 us
    all_gather x1, waiting for transfers between devices, local(): lax.all_gather(share, 'mp', axis=1, tiled=True)  98 us
    psum x1, blocking collectives, local(): total = lax.psum(objective, 'section')  57.4 us
  transfers between devices with their start and end apart: 7, of which 7 were waited for; matrix products, arithmetic and copies ran while one was open for 1% of the time, Pallas kernels for 0%

commit v1 on v0

v1 whole, which is shorter than its diff:
```python
import functools

import jax
import jax.numpy as jnp
from jax import lax
from jax.experimental import pallas as pl
from jax.experimental.pallas import tpu as pltpu
from jax.sharding import PartitionSpec as P

F32 = jnp.float32
BF16 = jnp.bfloat16
MESH = pl.DeviceIdType.MESH

X, Z, Y = 4, 4, 4
ZL, CORES = 4, 2


def round_up(value, step):
    return (value + step - 1) // step * step


def kernel(
    dims,
    table,
    pend,
    arriving,
    teacher,
    mapping,
    gain,
    gate,
    low,
    grad_gate,
    grad_down,
    loss,
    gz,
    full,
    part,
    tpart,
    r1,
    t1,
    s1,
    u1,
    r2,
    t2,
    zs,
    tz,
    r3,
    t3,
    share,
    nat,
    gain_cols,
    low_nat,
    low_rows,
    map_all,
    map_nat,
    map_rows,
    sel_out,
    sel_own,
    sel_in,
    sel_far,
    normed,
    delta,
    act,
    gsum,
    slope,
    lz,
    lx,
    ly,
    ll,
    lc,
    send_sem,
    recv_sem,
):
    width, rows, tokens, ff = dims
    pad = round_up(rows, 16)
    half = Z // 2
    long = half * rows
    sections = ZL * CORES
    sec, mp = lax.axis_index("section"), lax.axis_index("mp")
    x, z, y = mp // (Z * Y), mp // Y % Z, mp % Y
    zl, core = sec // CORES, sec % CORES

    def at_x(d):
        return (sec, lax.rem(x + d, X) * (Z * Y) + z * Y + y)

    def at_z(d):
        return (sec, x * (Z * Y) + lax.rem(z + d, Z) * Y + y)

    def at_y(d):
        return (sec, x * (Z * Y) + z * Y + lax.rem(y + d, Y))

    def at_zl(d):
        return (lax.rem(zl + d, ZL) * CORES + core, mp)

    sibling = (zl * CORES + 1 - core, mp)
    following = (lax.rem(sec + 1, sections), mp)
    previous = (lax.rem(sec + sections - 1, sections), mp)

    firsts = (at_y, at_x)
    seconds = (at_x, at_y)
    coords = ((y, x), (x, y))

    used = [0]
    unsent = []

    def send(src, dst, device):
        k = used[0]
        used[0] += 1
        copy = pltpu.make_async_remote_copy(
            src_ref=src,
            dst_ref=dst,
            send_sem=send_sem.at[k],
            recv_sem=recv_sem.at[k],
            device_id=device,
            device_id_type=MESH,
        )
        copy.start()
        unsent.append(copy)
        return copy

    def arrived(copies):
        for copy in copies:
            copy.wait_recv()

    def flush():
        for copy in unsent:
            copy.wait_send()
        unsent.clear()

    def natural(h, i1, i2, k):
        bx, by = (i2, i1) if h == 0 else (i1, i2)
        return pl.multiple_of(((bx * Z + h * half + k) * Y + by) * rows, 8)

    def padded(values):
        if pad == rows:
            return values
        return jnp.concatenate([values, jnp.zeros((pad - rows, tokens), F32)], axis=0)

    def gather_z(a):
        return [send(gz.at[a, z], gz.at[a, z], at_z(d)) for d in range(1, Z)]

    def gather_first(a, copies):
        arrived(copies)
        near, far = [], []
        for h in range(2):
            block = jnp.concatenate(
                [gz[a, h * half + k].astype(F32)[:rows] for k in range(half)], axis=0
            )
            c1, c2 = coords[h]
            full[a, h, c1, c2] = block.astype(BF16)
        for h in range(2):
            c1, c2 = coords[h]
            ref = full.at[a, h, c1, c2]
            near.append([send(ref, ref, seconds[h](d)) for d in range(1, X)])
        for h in range(2):
            c1, c2 = coords[h]
            ref = full.at[a, h, c1, c2]
            far.extend(send(ref, ref, firsts[h](d)) for d in range(1, X))
        return near, far

    def gather_second(a, state):
        near, far = state
        for e in range(1, X):
            for h in range(2):
                near[h][e - 1].wait_recv()
                c1, c2 = coords[h]
                ref = full.at[a, h, c1, lax.rem(c2 + X - e, X)]
                far.extend(send(ref, ref, firsts[h](d)) for d in range(1, X))
        return far

    def reduce_first(src, dst):
        copies = [[], []]
        for d in range(1, X):
            for h in range(2):
                c1, _ = coords[h]
                copies[h].append(
                    send(src.at[h, lax.rem(c1 + d, X)], dst.at[h, d - 1], firsts[h](d))
                )
        return copies

    def reduce_second(src, got, sums, dst, copies):
        out = [[], []]
        for h in range(2):
            arrived(copies[h])
            c1, c2 = coords[h]
            for i in range(X):
                total = src[h, c1, i].astype(F32)
                for d in range(X - 1):
                    total = total + got[h, d, i].astype(F32)
                sums[h, i] = total.astype(BF16)
            for d in range(1, X):
                out[h].append(send(sums.at[h, lax.rem(c2 + d, X)], dst.at[h, d - 1], seconds[h](d)))
        return out

    def reduce_third(sums, got, dst, landing, copies, count):
        for h in range(2):
            arrived(copies[h])
            _, c2 = coords[h]
            total = sums[h, c2].astype(F32)
            for d in range(X - 1):
                total = total + got[h, d].astype(F32)
            for j in range(count):
                for k in range(half):
                    start = j * long + k * rows
                    piece = padded(total[start : start + rows])
                    dst[h * half + k, j * pad : (j + 1) * pad] = piece.astype(BF16)
        return [
            send(dst.at[lax.rem(z + d, Z)], landing.at[d - 1], at_z(d)) for d in range(1, Z)
        ]

    def reduce_end(src, got, copies):
        arrived(copies)
        total = src[z].astype(F32)
        for d in range(Z - 1):
            total = total + got[d].astype(F32)
        return total

    peers = [at_x(d) for d in range(1, X)] + [at_z(d) for d in range(1, Z)]
    peers += [at_y(d) for d in range(1, Y)] + [at_zl(d) for d in range(1, ZL)]
    peers += [sibling, following, previous]
    barrier = pltpu.get_barrier_semaphore()
    for peer in peers:
        pl.semaphore_signal(barrier, inc=1, device_id=peer, device_id_type=MESH)
    held_first = padded(pend[...].astype(F32))
    gz[0, z] = held_first.astype(BF16)
    map_all[sec] = mapping[...]
    zeros = jnp.zeros((2 * tokens, teacher.shape[2]), BF16)

    def chosen_for(to):
        local = teacher.shape[0]
        depth = table[to] - sec * local
        mine = jnp.logical_and(depth >= 0, depth < local)
        block = teacher[jnp.clip(depth, 0, local - 1)]
        return jnp.where(mine, block, zeros)

    for i in range(ZL):
        sel_out[i] = chosen_for(i * CORES + 1 - core)
        sel_own[i] = chosen_for(i * CORES + core)
    pl.semaphore_wait(barrier, len(peers))

    gathered = gather_z(0)
    sel_copy = send(sel_out, sel_in, sibling)
    map_copies = [send(map_all.at[sec], map_all.at[sec], at_zl(d)) for d in range(1, ZL)]
    map_other = [send(map_all.at[sec], map_all.at[sec], sibling)]

    state = gather_first(0, gathered)

    for c in range(width // 128):
        line = jnp.broadcast_to(gain[:, c * 128 : (c + 1) * 128], (128, 128))
        gain_cols[c * 128 : (c + 1) * 128, :] = line.T
        low_nat[c * 128 : (c + 1) * 128, :] = low[:, c * 128 : (c + 1) * 128].astype(F32).T

    far = gather_second(0, state)

    sel_copy.wait_recv()
    for i in range(ZL):
        sel_own[i] = sel_own[i] + sel_in[i]
    sel_copies = [
        send(sel_own.at[lax.rem(zl + d, ZL)], sel_far.at[d - 1], at_zl(d)) for d in range(1, ZL)
    ]

    def order_rows(src, dst):
        for h in range(2):
            for i1 in range(X):
                for i2 in range(X):
                    block = jnp.concatenate(
                        [src[pl.ds(natural(h, i1, i2, k), rows), :] for k in range(half)], axis=0
                    )
                    start = ((h * X + i1) * X + i2) * long
                    dst[start : start + long, :] = block.astype(BF16)

    order_rows(low_nat, low_rows)

    for e in range(1, ZL):
        map_copies[e - 1].wait_recv()
        ref = map_all.at[lax.rem(zl + ZL - e, ZL) * CORES + core]
        map_other.append(send(ref, ref, sibling))

    def assemble(a):
        square = jnp.zeros((8, tokens), F32)
        for h in range(2):
            for i1 in range(X):
                for i2 in range(X):
                    block = full[a, h, i1, i2].astype(F32)
                    square = square + jnp.sum((block * block).reshape(-1, 8, tokens), axis=0)
                    for k in range(half):
                        start = natural(h, i1, i2, k)
                        nat[pl.ds(start, rows), :] = block[k * rows : (k + 1) * rows]
        return square

    def forward(t, a):
        square = assemble(a)
        spread = jnp.sum(square, axis=0, keepdims=True) / width
        factor = lax.rsqrt(spread + 1e-06)
        lanes = slice(t * tokens, (t + 1) * tokens)
        step = 128
        for c in range(width // step):
            block = slice(c * step, (c + 1) * step)
            normed[block, lanes] = (nat[block, :] * factor * gain_cols[block, :]).astype(BF16)
        gate_sum = jnp.dot(gate[...], normed[:, lanes], preferred_element_type=F32)
        gsum[t] = gate_sum
        activated = (gate_sum * (1.0 / (1.0 + jnp.exp(-gate_sum)))).astype(BF16)
        act[:, lanes] = activated
        size = X * X * long
        for h in range(2):
            for i1 in range(X):
                start = (h * X + i1) * X * long
                got = jnp.dot(
                    low_rows[start : start + X * long, :], activated, preferred_element_type=F32
                )
                part[t, h, i1] = got.astype(BF16).reshape(X, long, tokens)

    arrived(far)
    forward(0, 0)
    reduced = reduce_first(part.at[0], r1.at[0])

    arrived(sel_copies)
    chosen = sel_own[zl]
    for d in range(ZL - 1):
        chosen = chosen + sel_far[d]
    arrived(map_other)
    for s in range(sections):
        rows_of = map_all.shape[1]
        map_nat[s * rows_of : (s + 1) * rows_of, :] = map_all[s].astype(F32)
    order_rows(map_nat, map_rows)
    for h in range(2):
        for i1 in range(X):
            start = (h * X + i1) * X * long
            for t in range(2):
                got = lax.dot_general(
                    map_rows[start : start + X * long, :],
                    chosen[t * tokens : (t + 1) * tokens],
                    (((1,), (1,)), ((), ())),
                    preferred_element_type=F32,
                )
                tpart[h, i1, :, t * long : (t + 1) * long, :] = got.astype(BF16).reshape(
                    X, long, tokens
                )
    treduced = reduce_first(tpart, t1)

    reduced = reduce_second(part.at[0], r1.at[0], s1.at[0], r2.at[0], reduced)
    reduced = reduce_third(s1.at[0], r2.at[0], zs.at[0], r3.at[0], reduced, 1)
    mixed = reduce_end(zs.at[0], r3.at[0], reduced)
    output0 = (held_first.astype(F32) + mixed).astype(BF16)
    share[0] = output0
    passed = send(share.at[0], share.at[1], following)
    passed.wait_recv()
    entering = padded(arriving[...].astype(F32))
    held_second = jnp.where(sec == 0, entering, share[1].astype(F32))
    gz[1, z] = held_second.astype(BF16)
    gathered = gather_z(1)

    treduced = reduce_second(tpart, t1, u1, t2, treduced)
    state = gather_first(1, gathered)
    far = gather_second(1, state)
    treduced = reduce_third(u1, t2, tz, t3, treduced, 2)
    flush()
    arrived(far)
    forward(1, 1)
    reduced = reduce_first(part.at[1], r1.at[1])

    def differ_of(output, target):
        return output.astype(F32) - target.astype(F32)

    target = reduce_end(tz, t3, treduced).astype(BF16)
    differ0 = differ_of(share[0], target[:pad])
    gz[2, z] = (differ0 / tokens).astype(BF16)
    gathered0 = gather_z(2)
    reduced = reduce_second(part.at[1], r1.at[1], s1.at[1], r2.at[1], reduced)
    state0 = gather_first(2, gathered0)
    reduced = reduce_third(s1.at[1], r2.at[1], zs.at[1], r3.at[1], reduced, 1)
    far0 = gather_second(2, state0)
    mixed = reduce_end(zs.at[1], r3.at[1], reduced)
    output1 = (held_second + mixed).astype(BF16)
    differ1 = differ_of(output1, target[pad:])
    gz[3, z] = (differ1 / tokens).astype(BF16)
    gathered1 = gather_z(3)

    square = differ0 * differ0 + differ1 * differ1
    square = jnp.sum(square.reshape(-1, 8, tokens), axis=0)

    def exchange(buffer, mine, values, sends):
        buffer[mine] = values
        return [send(buffer.at[mine], buffer.at[mine], device) for device in sends]

    def summed(buffer, copies):
        arrived(copies)
        total = buffer[0]
        for i in range(1, buffer.shape[0]):
            total = total + buffer[i]
        return total

    loss_copies = exchange(lz, z, square, [at_z(d) for d in range(1, Z)])

    def assemble_delta(t, a):
        lanes = slice(t * tokens, (t + 1) * tokens)
        assemble(a)
        step = 128
        for c in range(width // step):
            block = slice(c * step, (c + 1) * step)
            delta[block, lanes] = nat[block, :].astype(BF16)

    def backward(t):
        lanes = slice(t * tokens, (t + 1) * tokens)
        back = jnp.dot(low[...], delta[:, lanes], preferred_element_type=F32)
        gate_sum = gsum[t]
        sigma = 1.0 / (1.0 + jnp.exp(-gate_sum))
        slope[:, lanes] = (back * sigma * (1.0 + gate_sum * (1.0 - sigma))).astype(BF16)

    state1 = gather_first(3, gathered1)
    square = summed(lz, loss_copies)
    loss_copies = exchange(lx, x, square, [at_x(d) for d in range(1, X)])
    far1 = gather_second(3, state1)
    square = summed(lx, loss_copies)
    loss_copies = exchange(ly, y, square, [at_y(d) for d in range(1, Y)])
    arrived(far0)
    assemble_delta(0, 2)
    backward(0)
    square = summed(ly, loss_copies)
    loss_copies = exchange(ll, zl, square, [at_zl(d) for d in range(1, ZL)])
    flush()
    square = summed(ll, loss_copies)
    loss_copies = exchange(lc, core, square, [sibling])
    arrived(far1)
    assemble_delta(1, 3)
    backward(1)
    turned = (((1,), (1,)), ((), ()))
    step = 512 if width % 512 == 0 else 128
    for c in range(width // step):
        block = slice(c * step, (c + 1) * step)
        got = lax.dot_general(slope[...], normed[block, :], turned, preferred_element_type=F32)
        grad_gate[:, block] = got.astype(BF16)
        got = lax.dot_general(act[...], delta[block, :], turned, preferred_element_type=F32)
        grad_down[:, block] = got.astype(BF16)
    square = summed(lc, loss_copies)
    objective = jnp.sum(square) / (2.0 * tokens)
    loss[0, 0] = objective / (sections * 2 * width)
    flush()


def copies_needed():
    gather = (Z - 1) + 2 * (X - 1) + 2 * (X - 1) + 2 * (X - 1) * (X - 1)
    reduce = 4 * (X - 1) + (Z - 1)
    section = 1 + (ZL - 1) + (ZL - 1) + ZL + 1
    loss = (Z - 1) + (X - 1) + (Y - 1) + (ZL - 1) + 1
    return 4 * gather + 3 * reduce + section + loss


def local(
    pending_vectors,
    arriving_learner_vectors,
    mentor_state_vectors,
    breadth_mapping_matrix,
    rms_gain_factor,
    gating_matrix,
    lowering_matrix,
    mentor_depth_table,
):
    width = gating_matrix.shape[1]
    ff = gating_matrix.shape[2]
    tokens, rows = pending_vectors.shape[1:]
    depths, feats = mentor_state_vectors.shape[0], mentor_state_vectors.shape[3]
    pad = round_up(rows, 16)
    long = Z // 2 * rows
    columns = breadth_mapping_matrix.shape[1]
    vmem = pl.BlockSpec(memory_space=pltpu.VMEM)
    smem = pl.BlockSpec(memory_space=pltpu.SMEM)
    copies = copies_needed()
    scratch = [
        pltpu.VMEM((4, Z, pad, tokens), BF16),
        pltpu.VMEM((4, 2, X, X, long, tokens), BF16),
        pltpu.VMEM((2, 2, X, X, long, tokens), BF16),
        pltpu.VMEM((2, X, X, 2 * long, tokens), BF16),
        pltpu.VMEM((2, 2, X - 1, X, long, tokens), BF16),
        pltpu.VMEM((2, X - 1, X, 2 * long, tokens), BF16),
        pltpu.VMEM((2, 2, X, long, tokens), BF16),
        pltpu.VMEM((2, X, 2 * long, tokens), BF16),
        pltpu.VMEM((2, 2, X - 1, long, tokens), BF16),
        pltpu.VMEM((2, X - 1, 2 * long, tokens), BF16),
        pltpu.VMEM((2, Z, pad, tokens), BF16),
        pltpu.VMEM((Z, 2 * pad, tokens), BF16),
        pltpu.VMEM((2, Z - 1, pad, tokens), BF16),
        pltpu.VMEM((Z - 1, 2 * pad, tokens), BF16),
        pltpu.VMEM((2, pad, tokens), BF16),
        pltpu.VMEM((width, tokens), F32),
        pltpu.VMEM((width, tokens), F32),
        pltpu.VMEM((width, ff), F32),
        pltpu.VMEM((width, ff), BF16),
        pltpu.VMEM((ZL * CORES, columns, feats), BF16),
        pltpu.VMEM((width, feats), F32),
        pltpu.VMEM((width, feats), BF16),
        pltpu.VMEM((ZL, 2 * tokens, feats), BF16),
        pltpu.VMEM((ZL, 2 * tokens, feats), BF16),
        pltpu.VMEM((ZL, 2 * tokens, feats), BF16),
        pltpu.VMEM((ZL - 1, 2 * tokens, feats), BF16),
        pltpu.VMEM((width, 2 * tokens), BF16),
        pltpu.VMEM((width, 2 * tokens), BF16),
        pltpu.VMEM((ff, 2 * tokens), BF16),
        pltpu.VMEM((2, ff, tokens), F32),
        pltpu.VMEM((ff, 2 * tokens), BF16),
        pltpu.VMEM((Z, 8, tokens), F32),
        pltpu.VMEM((X, 8, tokens), F32),
        pltpu.VMEM((Y, 8, tokens), F32),
        pltpu.VMEM((ZL, 8, tokens), F32),
        pltpu.VMEM((CORES, 8, tokens), F32),
        pltpu.SemaphoreType.DMA((copies,)),
        pltpu.SemaphoreType.DMA((copies,)),
    ]
    grad_gate, grad_down, loss = pl.pallas_call(
        functools.partial(kernel, (width, rows, tokens, ff)),
        out_shape=(
            jax.ShapeDtypeStruct((ff, width), BF16),
            jax.ShapeDtypeStruct((ff, width), BF16),
            jax.ShapeDtypeStruct((1, 1), F32),
        ),
        in_specs=[smem] + [vmem] * 7,
        out_specs=(vmem, vmem, smem),
        scratch_shapes=scratch,
        compiler_params=pltpu.CompilerParams(
            collective_id=0, has_side_effects=True, vmem_limit_bytes=56 * 1024 * 1024
        ),
    )(
        mentor_depth_table,
        pending_vectors[0].T,
        arriving_learner_vectors[0].T,
        mentor_state_vectors.reshape(depths, 2 * tokens, feats),
        breadth_mapping_matrix.T,
        rms_gain_factor,
        gating_matrix[0].T,
        lowering_matrix[0],
    )
    return grad_gate.T[None], grad_down[None], loss[0, 0]


def solution(mesh):
    in_specs = (
        P("section", None, "mp"),
        P(None, None, "mp"),
        P("section", None, None, "mp"),
        P("mp", "section"),
        P("section", None),
        P("section", None, "mp"),
        P("section", "mp", None),
        P(),
    )
    out_specs = (P("section", None, "mp"), P("section", "mp", None), P())
    return jax.shard_map(local, mesh=mesh, in_specs=in_specs, out_specs=out_specs, check_vma=False)
```

time: 2480 us -> 134 us (0.05)
  waiting for transfers between devices: 2280 us -> 0 us
  Pallas kernels: 0 us -> 128 us
  blocking collectives: 80.3 us -> 0 us
  starting transfers between devices: 45.3 us -> 0 us
  matrix products: 28.4 us -> 0 us
    psum x2 -> x0, waiting for transfers between devices: 1570 us -> none  [local(): mixed = lax.psum(partial_out, 'mp')]
    unnamed x7 -> x0, waiting for transfers between devices: 405 us -> none
    all_gather x3 -> x0, waiting for transfers between devices: 295 us -> none  [the longest x1 156 us: local(): entering = lax.all_gather(is_opening, 'mp', axis=2, tiled=True)]
    pallas_call x0 -> x1, Pallas kernels: none -> 128 us  [local(): pl.pallas_call(functools.partial(kernel, (width, rows, tokens, ff)), out_...]
    psum x1 -> x0, blocking collectives: 57.4 us -> none  [local(): total = lax.psum(objective, 'section')]
    ppermute x1 -> x0, starting transfers between devices: 45.1 us -> none  [shifted(): return lax.ppermute(shard, axis, pairs)]
    dot_general x9 -> x0, matrix products: 26 us -> none  [the longest x2 8.5 us: local(): jnp.dot(normed.T, slope, preferred_element_type=jnp.float32)]
  transfers between devices with their start and end apart: 7 -> 0, of which waited for: 7 -> 0; matrix products, arithmetic and copies ran while one was open for 1% -> 0% of each run, Pallas kernels for 0% -> 0%
where the time goes in v1:
time: 134 us
  Pallas kernels  128 us (96%)
  local copies, waits for them, and re-layouts  3.37 us (3%)
  between operations  2.46 us (2%)
    pallas_call x1, Pallas kernels, local(): pl.pallas_call(functools.partial(kernel, (width, rows, tokens, ff)), out_...  128 us
    unnamed x4, local copies, waits for them, and re-layouts  3.37 us

profile of v1, /device:TPU:1, one launch (start us, length us, event | category | flops | bytes accessed | tf_op | source)
XLA Modules:
  0.0 133.6 jit_solution(5709364061670719175)
XLA Ops:
  0.6 127.8 %shard_map.103 = (bf16[148,3584]{1,0:T(8,128)(2,1)}, bf16[148,3584]{1,0:T(8,128)(2,1)}, f32[1,1]{1,0:T(1,128)}) custom-call(s32[8]{0:T(128)} %table.1, bf16[56,128]{1,0:T(8,128)(2,1)} %bitcast.23, bf16[56,128]{1,0:T(8,128)(2,1)} %bitcast.24, bf16[8,256,128]{2,1,0:T(8,128)(2,1)} %bitcast.21, bf16[448,128]{1,0:T(8,128)(2,1)} %bitcast.22, f32[1,3584]{1,0:T(1,128)} %gain.1, ...), custom_call_target="tpu_custom_call" | custom-call | tf_op jit(solution)/shard_map/pallas_call | solution.py:509
  128.4 0.0 copy-start
  128.4 2.4 %copy.14 = bf16[1,3584,148]{1,2,0:T(8,128)(2,1)} copy(bf16[1,3584,148]{1,2,0:T(8,128)(2,1)} %bitcast.18) | data formatting | bytes 2121728
  130.8 0.0 copy-done
  130.8 1.0 copy.15
Async XLA Ops:
  128.4 2.4 %copy-start = (bf16[148,3584]{1,0:T(8,128)(2,1)S(1)}, bf16[148,3584]{1,0:T(8,128)(2,1)}, u32[]{:S(2)}) copy-start(bf16[148,3584]{1,0:T(8,128)(2,1)} %get-tuple-element.7) | copy-start | bytes 3182596

commit v2 on v1

v2 whole, which is shorter than its diff:
```python
import functools

import jax
import jax.numpy as jnp
from jax import lax
from jax.experimental import pallas as pl
from jax.experimental.pallas import tpu as pltpu
from jax.sharding import PartitionSpec as P

F32 = jnp.float32
BF16 = jnp.bfloat16
MESH = pl.DeviceIdType.MESH

X, Z, Y = 4, 4, 4
ZL, CORES = 4, 2


def round_up(value, step):
    return (value + step - 1) // step * step


def kernel(
    dims,
    table,
    pend,
    arriving,
    teacher,
    mapping,
    gain,
    gate,
    low,
    grad_gate,
    grad_down,
    loss,
    gz,
    came,
    full,
    part,
    tpart,
    r1,
    t1,
    s1,
    u1,
    r2,
    t2,
    zs,
    tz,
    share,
    nat,
    gain_cols,
    low_nat,
    low_rows,
    map_all,
    map_rows,
    sel_out,
    sel_own,
    sel_in,
    sel_far,
    normed,
    delta,
    act,
    gsum,
    slope,
    lx,
    ly,
    lc,
    send_sem,
    recv_sem,
):
    width, rows, tokens, ff = dims
    pad = round_up(rows, 16)
    half = Z // 2
    long = half * rows
    sections = ZL * CORES
    sec, mp = lax.axis_index("section"), lax.axis_index("mp")
    x, z, y = mp // (Z * Y), mp // Y % Z, mp % Y
    zl, core = sec // CORES, sec % CORES

    def at_x(d):
        return (sec, lax.rem(x + d, X) * (Z * Y) + z * Y + y)

    def at_z(d):
        return (sec, x * (Z * Y) + lax.rem(z + d, Z) * Y + y)

    def at_y(d):
        return (sec, x * (Z * Y) + z * Y + lax.rem(y + d, Y))

    def at_zl(d):
        return (lax.rem(zl + d, ZL) * CORES + core, mp)

    sibling = (zl * CORES + 1 - core, mp)

    firsts = (at_y, at_x)
    seconds = (at_x, at_y)
    coords = ((y, x), (x, y))
    away = range(1, X)

    def at_section(d):
        return (lax.rem(sec + d, sections), mp)

    def at_next(peer):
        return (lax.rem(sec + 1, sections), peer[1])

    def at_previous(peer):
        return (lax.rem(sec + sections - 1, sections), peer[1])

    used = [0]
    unsent = []

    def send(src, dst, device):
        k = used[0]
        used[0] += 1
        copy = pltpu.make_async_remote_copy(
            src_ref=src,
            dst_ref=dst,
            send_sem=send_sem.at[k],
            recv_sem=recv_sem.at[k],
            device_id=device,
            device_id_type=MESH,
        )
        copy.start()
        unsent.append(copy)
        return copy

    def arrived(copies):
        for copy in copies:
            copy.wait_recv()

    def flush():
        for copy in unsent:
            copy.wait_send()
        unsent.clear()

    def natural(h, i1, i2, k):
        bx, by = (i2, i1) if h == 0 else (i1, i2)
        return pl.multiple_of(((bx * Z + h * half + k) * Y + by) * rows, 8)

    def padded(values):
        if pad == rows:
            return values
        return jnp.concatenate([values, jnp.zeros((pad - rows, tokens), F32)], axis=0)

    def line_start(b):
        return [send(gz.at[b, z], gz.at[b, z], at_z(d)) for d in range(1, Z)]

    def line_block(b, h):
        block = [gz[b, h * half + k].astype(F32)[:rows] for k in range(half)]
        return jnp.concatenate(block, axis=0).astype(BF16)

    def nothing():
        pass

    def gather_first(a):
        near, far = [[], []], []
        for d in away:
            for h in range(2):
                c1, c2 = coords[h]
                ref = full.at[a, h, c1, c2]
                near[h].append(send(ref, ref, seconds[h](d)))
        spread_out(a, 0, far)
        return near, far

    def spread_out(a, e, far):
        for d in range(1, X):
            for h in range(2):
                c1, c2 = coords[h]
                i2 = lax.rem(c2 + X - e, X)
                ref = full.at[a, h, c1, i2]
                far.append((send(ref, ref, firsts[h](d)), h, lax.rem(c1 + X - d, X), i2))

    def gather_second(a, state, also=nothing):
        near, far = state
        also()
        for e in range(1, X):
            for h in range(2):
                near[h][e - 1].wait_recv()
            spread_out(a, e, far)
        return far

    def gather_end(a, far):
        square = jnp.zeros((8, tokens), F32)

        def place(h, i1, i2, square):
            block = full[a, h, i1, i2].astype(F32)
            for k in range(half):
                nat[pl.ds(natural(h, i1, i2, k), rows), :] = block[k * rows : (k + 1) * rows]
            return square + jnp.sum((block * block).reshape(-1, 8, tokens), axis=0)

        for h in range(2):
            c1, c2 = coords[h]
            for e in range(X):
                square = place(h, c1, lax.rem(c2 + X - e, X), square)
        for copy, h, i1, i2 in far:
            copy.wait_recv()
            square = place(h, i1, i2, square)
        return square

    first_part, last_part = pl.ds(1, X // 2), pl.ds(X // 2 + 1, X // 2 - 1)

    def reduce_first(compute, src, dst):
        early, late, own = [[], []], [[], []], [[], []]
        for d in range(1, X):
            for h in range(2):
                compute(h, d)
                for refs, span in ((early, first_part), (late, last_part)):
                    if span.size:
                        refs[h].append(
                            send(src.at[h, d, span], dst.at[h, d - 1, span], firsts[h](d))
                        )
        for d in range(1, X):
            for h in range(2):
                own[h].append(send(src.at[h, d, 0], dst.at[h, d - 1, 0], firsts[h](d)))
        for h in range(2):
            compute(h, 0)
        return early, late, own

    def reduce_second(src, got, sums, dst, copies):
        out = [[], []]
        spans = (
            range(1, X // 2 + 1),
            range(X // 2 + 1, X),
            range(1),
        )
        for span, group in zip(spans, copies):
            for h in range(2):
                arrived(group[h])
                for i in span:
                    total = src[h, 0, i].astype(F32)
                    for d in range(X - 1):
                        total = total + got[h, d, i].astype(F32)
                    sums[h, i] = total.astype(BF16)
                    if i:
                        out[h].append(send(sums.at[h, i], dst.at[h, i - 1], seconds[h](i)))
        return out

    def reduce_third(sums, got, lines, copies):
        out = []
        for h in range(2):
            arrived(copies[h])
            total = sums[h, 0].astype(F32)
            for d in range(X - 1):
                total = total + got[h, d].astype(F32)
            lines[z, h] = total.astype(BF16)
            ref = lines.at[z, h]
            out.extend(send(ref, ref, at_z(d)) for d in (2, 1, 3))
        return out

    def reduce_end(lines, copies):
        arrived(copies)
        total = lines[0].astype(F32)
        for i in range(1, Z):
            total = total + lines[i].astype(F32)
        return total

    beside = [at_x(d) for d in away] + [at_y(d) for d in away]
    peers = beside + [at_z(d) for d in range(1, Z)]
    peers += [at_section(d) for d in range(1, sections)]
    peers += [at_next(peer) for peer in beside] + [at_previous(peer) for peer in beside]
    barrier = pltpu.get_barrier_semaphore()
    for peer in peers:
        pl.semaphore_signal(barrier, inc=1, device_id=peer, device_id_type=MESH)
    gz[0, z] = padded(pend[...].astype(F32)).astype(BF16)
    gz[1, z] = padded(arriving[...].astype(F32)).astype(BF16)
    pl.semaphore_wait(barrier, len(peers))
    line0 = line_start(0)

    map_all[sec] = mapping[...]
    zeros = jnp.zeros((2 * tokens, teacher.shape[2]), BF16)

    def chosen_for(to):
        local = teacher.shape[0]
        depth = table[to] - sec * local
        mine = jnp.logical_and(depth >= 0, depth < local)
        block = teacher[jnp.clip(depth, 0, local - 1)]
        return jnp.where(mine, block, zeros)

    for i in range(ZL):
        sel_out[i] = chosen_for(i * CORES + 1 - core)
        sel_own[i] = chosen_for(i * CORES + core)
    sel_copy = send(sel_out, sel_in, sibling)
    for c in range(width // 128):
        low_nat[c * 128 : (c + 1) * 128, :] = low[:, c * 128 : (c + 1) * 128].astype(F32).T

    for c in range(width // 128):
        line = jnp.broadcast_to(gain[:, c * 128 : (c + 1) * 128], (128, 128))
        gain_cols[c * 128 : (c + 1) * 128, :] = line.T
    sel_copy.wait_recv()
    for i in range(ZL):
        sel_own[i] = sel_own[i] + sel_in[i]

    arrived(line0)
    for h in range(2):
        c1, c2 = coords[h]
        full[0, h, c1, c2] = line_block(0, h)
    state = gather_first(0)
    sel_copies = [
        send(sel_own.at[lax.rem(zl + d, ZL)], sel_far.at[d - 1], at_zl(d)) for d in range(1, ZL)
    ]
    map_copies = [send(map_all.at[sec], map_all.at[sec], at_zl(d)) for d in range(1, ZL)]
    map_other = [send(map_all.at[sec], map_all.at[sec], sibling)]
    line1 = line_start(1)
    far = gather_second(0, state)

    for h in range(2):
        c1, c2 = coords[h]
        for d1 in range(X):
            for d2 in range(X):
                i1, i2 = lax.rem(c1 + d1, X), lax.rem(c2 + d2, X)
                block = jnp.concatenate(
                    [low_nat[pl.ds(natural(h, i1, i2, k), rows), :] for k in range(half)], axis=0
                )
                low_rows[h, d1, d2 * long : (d2 + 1) * long, :] = block.astype(BF16)

    def forward(t, square):
        spread = jnp.sum(square, axis=0, keepdims=True) / width
        factor = lax.rsqrt(spread + 1e-06)
        lanes = slice(t * tokens, (t + 1) * tokens)
        step = 128
        for c in range(width // step):
            block = slice(c * step, (c + 1) * step)
            normed[block, lanes] = (nat[block, :] * factor * gain_cols[block, :]).astype(BF16)
        gate_sum = jnp.dot(gate[...], normed[:, lanes], preferred_element_type=F32)
        gsum[t] = gate_sum
        activated = (gate_sum * (1.0 / (1.0 + jnp.exp(-gate_sum)))).astype(BF16)
        act[:, lanes] = activated

        def lowered(h, d):
            got = jnp.dot(low_rows[h, d], activated, preferred_element_type=F32)
            part[t, h, d] = got.astype(BF16).reshape(X, long, tokens)

        return reduce_first(lowered, part.at[t], r1.at[t])

    reduced = forward(0, gather_end(0, far))
    reduced = reduce_second(part.at[0], r1.at[0], s1.at[0], r2.at[0], reduced)
    for e in range(1, ZL):
        map_copies[e - 1].wait_recv()
        ref = map_all.at[lax.rem(zl + ZL - e, ZL) * CORES + core]
        map_other.append(send(ref, ref, sibling))
    reduced = reduce_third(s1.at[0], r2.at[0], zs.at[0], reduced)

    arrived(line1)
    came_copies = []
    for h in range(2):
        _, c2 = coords[h]
        came[0, h, c2] = line_block(1, h)
        ref = came.at[0, h, c2]
        came_copies.extend(send(ref, ref, seconds[h](d)) for d in away)

    arrived(sel_copies)
    chosen = sel_own[zl]
    for d in range(ZL - 1):
        chosen = chosen + sel_far[d]
    arrived(map_other)
    for s in range(sections):
        i, h = s // CORES, s % CORES
        block = map_all[s].astype(F32)
        c1, c2 = coords[h]
        for j in range(Y):
            piece = jnp.concatenate(
                [block[(k * Y + j) * rows : (k * Y + j + 1) * rows] for k in range(half)], axis=0
            )
            i1, i2 = (j, i) if h == 0 else (i, j)
            d1, d2 = lax.rem(i1 + X - c1, X), lax.rem(i2 + X - c2, X)
            map_rows[h, d1, d2] = piece.astype(BF16)

    def targets(h, d):
        for t in range(2):
            got = lax.dot_general(
                map_rows[h, d].reshape(X * long, -1),
                chosen[t * tokens : (t + 1) * tokens],
                (((1,), (1,)), ((), ())),
                preferred_element_type=F32,
            )
            tpart[h, d, :, t * long : (t + 1) * long, :] = got.astype(BF16).reshape(
                X, long, tokens
            )

    treduced = reduce_first(targets, tpart, t1)

    def share_of(a):
        return jnp.stack([full[a, h, coords[h][0], coords[h][1]] for h in range(2)]).astype(F32)

    mixed = reduce_end(zs.at[0], reduced)
    share[...] = (share_of(0) + mixed).astype(BF16)
    passed = {}
    for d in range(X):
        for h in range(2):
            c2 = coords[h][1]
            peer = seconds[h](d) if d else (sec, mp)
            passed[h, d] = send(share.at[h], came.at[1, h, c2], at_next(peer))
    arrived(came_copies)
    far = []
    for e in range(X):
        for h in range(2):
            c1, c2 = coords[h]
            i2 = lax.rem(c2 + X - e, X)
            passed[h, e].wait_recv()
            full[1, h, c1, i2] = jnp.where(sec == 0, came[0, h, i2], came[1, h, i2])
        spread_out(1, e, far)
    treduced = reduce_second(tpart, t1, u1, t2, treduced)
    flush()
    treduced = reduce_third(u1, t2, tz, treduced)
    reduced = forward(1, gather_end(1, far))

    def differ_of(output, target):
        return output.astype(F32) - target.astype(F32)

    def start_delta(a, differ):
        for h in range(2):
            full[a, h, coords[h][0], coords[h][1]] = (differ[h] / tokens).astype(BF16)
        return gather_first(a)

    reduced = reduce_second(part.at[1], r1.at[1], s1.at[1], r2.at[1], reduced)
    reduced = reduce_third(s1.at[1], r2.at[1], zs.at[1], reduced)
    target = reduce_end(tz, treduced).astype(BF16)
    differ0 = differ_of(share[...], target[:, :long])
    state0 = start_delta(2, differ0)
    far0 = gather_second(2, state0)
    mixed = reduce_end(zs.at[1], reduced)
    output1 = (share_of(1) + mixed).astype(BF16)
    differ1 = differ_of(output1, target[:, long:])
    square = differ0 * differ0 + differ1 * differ1
    square = jnp.sum(square.reshape(-1, 8, tokens), axis=0)

    def exchange(buffer, mine, values, sends):
        buffer[mine] = values
        return [send(buffer.at[mine], buffer.at[mine], device) for device in sends]

    def summed(buffer, copies):
        arrived(copies)
        total = buffer[0]
        for i in range(1, buffer.shape[0]):
            total = total + buffer[i]
        return total

    loss_copies = [exchange(lx, x, square, [at_x(d) for d in away])]
    state1 = start_delta(3, differ1)

    def loss_y():
        values = summed(lx, loss_copies[0])
        loss_copies[0] = exchange(ly, y, values, [at_y(d) for d in away])

    def gather_delta(t, a, far):
        lanes = slice(t * tokens, (t + 1) * tokens)
        gather_end(a, far)
        step = 128
        for c in range(width // step):
            block = slice(c * step, (c + 1) * step)
            delta[block, lanes] = nat[block, :].astype(BF16)

    def backward(t):
        lanes = slice(t * tokens, (t + 1) * tokens)
        back = jnp.dot(low[...], delta[:, lanes], preferred_element_type=F32)
        gate_sum = gsum[t]
        sigma = 1.0 / (1.0 + jnp.exp(-gate_sum))
        slope[:, lanes] = (back * sigma * (1.0 + gate_sum * (1.0 - sigma))).astype(BF16)

    far1 = gather_second(3, state1, loss_y)
    values = summed(ly, loss_copies[0])
    loss_copies[0] = exchange(lc, sec, values, [at_section(d) for d in range(1, sections)])
    gather_delta(0, 2, far0)
    backward(0)
    flush()
    gather_delta(1, 3, far1)
    backward(1)
    turned = (((1,), (1,)), ((), ()))
    step = 512 if width % 512 == 0 else 128
    for c in range(width // step):
        block = slice(c * step, (c + 1) * step)
        got = lax.dot_general(slope[...], normed[block, :], turned, preferred_element_type=F32)
        grad_gate[:, block] = got.astype(BF16)
        got = lax.dot_general(act[...], delta[block, :], turned, preferred_element_type=F32)
        grad_down[:, block] = got.astype(BF16)
    square = summed(lc, loss_copies[0])
    objective = jnp.sum(square) / (2.0 * tokens)
    loss[0, 0] = objective / (sections * 2 * width)
    flush()


def copies_needed():
    line = 2 * (Z - 1)
    gather = 2 * X * (X - 1)
    near = 2 * (X - 1)
    reduce = 8 * (X - 1) + 2 * (Z - 1)
    section = 1 + (ZL - 1) + (ZL - 1) + ZL + 2 * X
    loss = (X - 1) + (Y - 1) + (ZL * CORES - 1)
    return line + 4 * (gather + near) + 3 * reduce + section + loss


def local(
    pending_vectors,
    arriving_learner_vectors,
    mentor_state_vectors,
    breadth_mapping_matrix,
    rms_gain_factor,
    gating_matrix,
    lowering_matrix,
    mentor_depth_table,
):
    width = gating_matrix.shape[1]
    ff = gating_matrix.shape[2]
    tokens, rows = pending_vectors.shape[1:]
    depths, feats = mentor_state_vectors.shape[0], mentor_state_vectors.shape[3]
    pad = round_up(rows, 16)
    long = Z // 2 * rows
    columns = breadth_mapping_matrix.shape[1]
    vmem = pl.BlockSpec(memory_space=pltpu.VMEM)
    smem = pl.BlockSpec(memory_space=pltpu.SMEM)
    copies = copies_needed()
    scratch = [
        pltpu.VMEM((2, Z, pad, tokens), BF16),
        pltpu.VMEM((2, 2, X, long, tokens), BF16),
        pltpu.VMEM((4, 2, X, X, long, tokens), BF16),
        pltpu.VMEM((2, 2, X, X, long, tokens), BF16),
        pltpu.VMEM((2, X, X, 2 * long, tokens), BF16),
        pltpu.VMEM((2, 2, X - 1, X, long, tokens), BF16),
        pltpu.VMEM((2, X - 1, X, 2 * long, tokens), BF16),
        pltpu.VMEM((2, 2, X, long, tokens), BF16),
        pltpu.VMEM((2, X, 2 * long, tokens), BF16),
        pltpu.VMEM((2, 2, X - 1, long, tokens), BF16),
        pltpu.VMEM((2, X - 1, 2 * long, tokens), BF16),
        pltpu.VMEM((2, Z, 2, long, tokens), BF16),
        pltpu.VMEM((Z, 2, 2 * long, tokens), BF16),
        pltpu.VMEM((2, long, tokens), BF16),
        pltpu.VMEM((width, tokens), F32),
        pltpu.VMEM((width, tokens), F32),
        pltpu.VMEM((width, ff), F32),
        pltpu.VMEM((2, X, X * long, ff), BF16),
        pltpu.VMEM((ZL * CORES, columns, feats), BF16),
        pltpu.VMEM((2, X, X, long, feats), BF16),
        pltpu.VMEM((ZL, 2 * tokens, feats), BF16),
        pltpu.VMEM((ZL, 2 * tokens, feats), BF16),
        pltpu.VMEM((ZL, 2 * tokens, feats), BF16),
        pltpu.VMEM((ZL - 1, 2 * tokens, feats), BF16),
        pltpu.VMEM((width, 2 * tokens), BF16),
        pltpu.VMEM((width, 2 * tokens), BF16),
        pltpu.VMEM((ff, 2 * tokens), BF16),
        pltpu.VMEM((2, ff, tokens), F32),
        pltpu.VMEM((ff, 2 * tokens), BF16),
        pltpu.VMEM((X, 8, tokens), F32),
        pltpu.VMEM((Y, 8, tokens), F32),
        pltpu.VMEM((ZL * CORES, 8, tokens), F32),
        pltpu.SemaphoreType.DMA((copies,)),
        pltpu.SemaphoreType.DMA((copies,)),
    ]
    grad_gate, grad_down, loss = pl.pallas_call(
        functools.partial(kernel, (width, rows, tokens, ff)),
        out_shape=(
            jax.ShapeDtypeStruct((ff, width), BF16),
            jax.ShapeDtypeStruct((ff, width), BF16),
            jax.ShapeDtypeStruct((1, 1), F32),
        ),
        in_specs=[smem] + [vmem] * 7,
        out_specs=(vmem, vmem, smem),
        scratch_shapes=scratch,
        compiler_params=pltpu.CompilerParams(
            collective_id=0, has_side_effects=True, vmem_limit_bytes=56 * 1024 * 1024
        ),
    )(
        mentor_depth_table,
        pending_vectors[0].T,
        arriving_learner_vectors[0].T,
        mentor_state_vectors.reshape(depths, 2 * tokens, feats),
        breadth_mapping_matrix.T,
        rms_gain_factor,
        gating_matrix[0].T,
        lowering_matrix[0],
    )
    return grad_gate.T[None], grad_down[None], loss[0, 0]


def solution(mesh):
    in_specs = (
        P("section", None, "mp"),
        P(None, None, "mp"),
        P("section", None, None, "mp"),
        P("mp", "section"),
        P("section", None),
        P("section", None, "mp"),
        P("section", "mp", None),
        P(),
    )
    out_specs = (P("section", None, "mp"), P("section", "mp", None), P())
    return jax.shard_map(local, mesh=mesh, in_specs=in_specs, out_specs=out_specs, check_vma=False)
```

time: 134 us -> 131 us (0.978)
  Pallas kernels: 128 us -> 125 us
    pallas_call x1, Pallas kernels: 128 us -> 125 us  [local(): pl.pallas_call(functools.partial(kernel, (width, rows, tokens, ff)), out_...]
where the time goes in v2:
time: 131 us
  Pallas kernels  125 us (95%)
  local copies, waits for them, and re-layouts  3.37 us (3%)
  between operations  2.46 us (2%)
    pallas_call x1, Pallas kernels, local(): pl.pallas_call(functools.partial(kernel, (width, rows, tokens, ff)), out_...  125 us
    unnamed x4, local copies, waits for them, and re-layouts  3.37 us

profile of v2, /device:TPU:1, one launch (start us, length us, event | category | flops | bytes accessed | tf_op | source)
XLA Modules:
  0.0 130.8 jit_solution(14455023796124446122)
XLA Ops:
  0.6 124.9 %shard_map.103 = (bf16[148,3584]{1,0:T(8,128)(2,1)}, bf16[148,3584]{1,0:T(8,128)(2,1)}, f32[1,1]{1,0:T(1,128)}) custom-call(s32[8]{0:T(128)} %table.1, bf16[56,128]{1,0:T(8,128)(2,1)} %bitcast.23, bf16[56,128]{1,0:T(8,128)(2,1)} %bitcast.24, bf16[8,256,128]{2,1,0:T(8,128)(2,1)} %bitcast.21, bf16[448,128]{1,0:T(8,128)(2,1)} %bitcast.22, f32[1,3584]{1,0:T(1,128)} %gain.1, ...), custom_call_target="tpu_custom_call" | custom-call | tf_op jit(solution)/shard_map/pallas_call | solution.py:546
  125.6 0.0 copy-start
  125.6 2.4 %copy.14 = bf16[1,3584,148]{1,2,0:T(8,128)(2,1)} copy(bf16[1,3584,148]{1,2,0:T(8,128)(2,1)} %bitcast.18) | data formatting | bytes 2121728
  128.0 0.0 copy-done
  128.0 1.0 copy.15
Async XLA Ops:
  125.6 2.4 %copy-start = (bf16[148,3584]{1,0:T(8,128)(2,1)S(1)}, bf16[148,3584]{1,0:T(8,128)(2,1)}, u32[]{:S(2)}) copy-start(bf16[148,3584]{1,0:T(8,128)(2,1)} %get-tuple-element.7) | copy-start | bytes 3182596
